TPU v7x, 512 devices: a whole 4x4x16 slice. The times are simulated.
512 devices in a mesh: inner: 32 (over x, y, core), outer: 16 (over z).
Axes of the slice: x: 4, y: 4, z: 16, core: 2. Of those that a mesh axis runs over, the one named last changes fastest.
Arguments:
- activations: bfloat16 [393216, 768], P(('inner', 'outer')), may hold values from -6 to 6
- out_grads: bfloat16 [393216, 768], P(('inner', 'outer')), may hold values from -0.016 to 0.016
- error_in: bfloat16 [512, 768, 768], P(('inner', 'outer')), may hold values from -4 to 4
- q_init: float32 [768, 8], replicated, may hold values from -6 to 6
Outputs:
- error_out: bfloat16 [512, 768, 768], P(('inner', 'outer'))
- p_basis: float32 [768, 8], replicated
- q_factor: float32 [768, 8], replicated
All inputs are finite; a program needn't handle non-finite values.
Results may differ from a plain program's by a relative error of at most 0.0012.
Values sent between devices are 32-bit elements; how exact they have to be, the bound alone decides.
No kernel may reach another device: no remote copies, remote signals or barrier semaphores. Data moves between devices by JAX's collectives and lax.ppermute only.
A program may use at most 64 MiB of HBM per device.

v0:
```python
import jax
import jax.numpy as jnp
from jax import lax
from jax.sharding import PartitionSpec as P

precision_mode = lax.Precision.HIGHEST


def normalize(factor, gram_matrix):
    lower_factor = jnp.linalg.cholesky(gram_matrix)
    return lax.linalg.triangular_solve(
        lower_factor, factor, left_side=False, lower=True, transpose_a=True
    )


def local(activations, out_grads, error_in, q_init):
    devices_all = lax.axis_size("inner") * lax.axis_size("outer")
    gradient = lax.dot_general(
        activations, out_grads, (((0,), (0,)), ((), ())), preferred_element_type=jnp.float32
    )
    merged = gradient + error_in[0].astype(jnp.float32)
    local_p = jnp.dot(merged, q_init, precision=precision_mode)
    p_sum = lax.psum(local_p, ("inner", "outer"))
    gram_matrix = jnp.dot(p_sum.T, p_sum, precision=precision_mode)
    p_basis = normalize(p_sum, gram_matrix)
    local_q = lax.dot_general(merged, p_basis, (((0,), (0,)), ((), ())), precision=precision_mode)
    group_q = lax.psum(local_q, "inner")
    q_factor = lax.psum(group_q, "outer")
    correction = jnp.dot(p_basis, q_factor.T, precision=precision_mode) / devices_all
    error_out = (merged - correction).astype(jnp.bfloat16)[None]
    return (error_out, p_basis, q_factor)


def solution(mesh):
    placed = (
        P(("inner", "outer"), None),
        P(("inner", "outer"), None),
        P(("inner", "outer"), None, None),
        P(),
    )
    return jax.shard_map(
        local,
        mesh=mesh,
        in_specs=placed,
        out_specs=(P(("inner", "outer"), None, None), P(), P()),
        check_vma=False,
    )
```

profile of v0, /device:TPU:32, one launch (start us, length us, event | category | flops | bytes accessed | tf_op | source)
XLA Modules:
  0.0 305.6 jit_solution(6047645002172566911)
XLA Ops:
  0.6 0.0 copy-start
  0.6 0.0 copy-start.2
  0.7 1.3 copy-done
  1.9 2.7 convert_add_fusion
  4.7 0.0 copy-done.2
  4.7 2.7 fusion.5
  7.3 109.6 %psum.21 = f32[768,8]{0,1:T(8,128)} all-reduce(f32[768,8]{0,1:T(8,128)} %fusion.5), channel_id=1, replica_groups=mesh['inner'=32,'outer'=16] {'inner','outer'}, use_global_device_ids=true, to_apply=%region_0.0 | all-reduce | flops 6144 | bytes 49152 | tf_op jit(solution)/shard_map/psum | solution.py:23
  116.9 1.0 fusion.6
  117.9 0.1 copy.7
  117.9 0.7 cholesky.16
  118.7 0.1 select_reduce_fusion
  118.7 0.6 compare_reduce_fusion
  119.4 0.6 fusion.1
  120.0 0.6 custom-call.6
  120.6 1.0 fusion.2
  121.6 0.0 copy-start.1
  121.6 0.6 copy-done.1
  122.2 1.9 fusion.7
  124.2 124.5 %psum.22 = f32[768,8]{0,1:T(8,128)} all-reduce(f32[768,8]{0,1:T(8,128)} %fusion.7), channel_id=1, replica_groups=mesh['inner'=32,'outer'=16] {'inner'}, use_global_device_ids=true, to_apply=%region_3.4 | all-reduce | flops 6144 | bytes 49152 | tf_op jit(solution)/shard_map/psum | solution.py:27
  248.7 53.0 %psum.23 = f32[768,8]{0,1:T(8,128)} all-reduce(f32[768,8]{0,1:T(8,128)} %psum.22), channel_id=1, replica_groups=mesh['inner'=32,'outer'=16] {'outer'}, use_global_device_ids=true, to_apply=%region_4.5 | all-reduce | flops 6144 | bytes 49152 | tf_op jit(solution)/shard_map/psum | solution.py:28
  301.7 3.9 %fusion = bf16[1,768,768]{2,1,0:T(8,128)(2,1)} fusion(f32[768,768]{1,0:T(8,128)S(1)} %convert_add_fusion, f32[768,8]{0,1:T(8,128)} %copy-done.1, f32[768,8]{0,1:T(8,128)} %psum.23), kind=kOutput, calls=%fused_computation.2 | convolution fusion | flops 58392576 | bytes 3588096 | tf_op jit(solution)/shard_map/dot_general | solution.py:29
  (1 shorter events, 0.0 us)
Async XLA Ops:
  0.6 1.3 copy-start
  0.6 4.0 %copy-start.2 = (f32[768,8]{0,1:T(8,128)S(1)}, f32[768,8]{0,1:T(8,128)}, u32[]{:S(2)}) copy-start(f32[768,8]{0,1:T(8,128)} %param.7) | copy-start | bytes 73732
  121.6 0.6 copy-start.1
where the time goes:
time: 306 us
  blocking collectives  287 us (94%)
  matrix products  13.1 us (4%)
    psum x1, blocking collectives, local(): group_q = lax.psum(local_q, 'inner')  125 us
    psum x1, blocking collectives, local(): p_sum = lax.psum(local_p, ('inner', 'outer'))  110 us
    psum x1, blocking collectives, local(): q_factor = lax.psum(group_q, 'outer')  53 us

commit v1 on v0

v1 whole, which is shorter than its diff:
```python
import jax
import jax.numpy as jnp
from jax import lax
from jax.sharding import PartitionSpec as P

precision_mode = lax.Precision.HIGHEST


def normalize(factor, gram_matrix):
    lower_factor = jnp.linalg.cholesky(gram_matrix)
    return lax.linalg.triangular_solve(lower_factor, factor, left_side=True, lower=True)


def exchange(parts, axis, groups=None):
    return lax.all_to_all(parts, axis, 0, 0, axis_index_groups=groups)


def reduce_all(rows):
    n_inner, n_outer = lax.axis_size("inner"), lax.axis_size("outer")
    rank, width = rows.shape
    groups = [list(range(first, first + rank)) for first in range(0, n_inner, rank)]
    parts = jnp.broadcast_to(rows[None], (n_inner // rank, rank, width)).reshape(n_inner, 1, width)
    row = jnp.sum(exchange(parts, "inner"), axis=0)
    parts = jnp.broadcast_to(row[None], (n_outer, 1, width))
    row = jnp.sum(exchange(parts, "outer"), axis=0)
    parts = jnp.broadcast_to(row[None], (rank, 1, width))
    return exchange(parts, "inner", groups).reshape(rank, width)


def local(activations, out_grads, error_in, q_init):
    devices_all = lax.axis_size("inner") * lax.axis_size("outer")
    gradient = lax.dot_general(
        activations, out_grads, (((0,), (0,)), ((), ())), preferred_element_type=jnp.float32
    )
    merged = gradient + error_in[0].astype(jnp.float32)
    local_p = lax.dot_general(q_init, merged, (((0,), (1,)), ((), ())), precision=precision_mode)
    p_sum = reduce_all(local_p)
    gram_matrix = jnp.dot(p_sum, p_sum.T, precision=precision_mode)
    p_basis = normalize(p_sum, gram_matrix)
    local_q = jnp.dot(p_basis, merged, precision=precision_mode)
    q_factor = reduce_all(local_q)
    correction = lax.dot_general(
        p_basis, q_factor, (((0,), (0,)), ((), ())), precision=precision_mode
    ) / devices_all
    error_out = (merged - correction).astype(jnp.bfloat16)[None]
    return (error_out, p_basis.T, q_factor.T)


def solution(mesh):
    placed = (
        P(("inner", "outer"), None),
        P(("inner", "outer"), None),
        P(("inner", "outer"), None, None),
        P(),
    )
    return jax.shard_map(
        local,
        mesh=mesh,
        in_specs=placed,
        out_specs=(P(("inner", "outer"), None, None), P(), P()),
        check_vma=False,
    )
```

time: 306 us -> 114 us (0.37)
  the two profiles are of different devices: /device:TPU:32 before, /device:TPU:1 now
where the time goes in v1:
time: 114 us; the launch traced here: 113 us
  blocking collectives  87.3 us (77%)
  matrix products  11 us (10%)
  local copies, waits for them, and re-layouts  7.8 us (7%)
  other arithmetic  6.33 us (6%)
    all_to_all x6, blocking collectives, exchange(): return lax.all_to_all(parts, axis, 0, 0, axis_index_groups=groups)  87.3 us
    dot_general x1, matrix products, local(): lax.dot_general(p_basis, q_factor, (((0,), (0,)), ((), ())), precision=pr...  3.87 us
    reshape x2, local copies, waits for them, and re-layouts, reduce_all(): jnp.broadcast_to(rows[None], (n_inner // rank, rank, width))  3.23 us
    unnamed x9, local copies, waits for them, and re-layouts  3.09 us
    dot_general x1, matrix products, local(): lax.dot_general(activations, out_grads, (((0,), (0,)), ((), ())), preferr...  2.75 us

profile of v1, /device:TPU:1, one launch (start us, length us, event | category | flops | bytes accessed | tf_op | source)
XLA Modules:
  0.0 113.1 jit_solution(1603297326703617944)
XLA Ops:
  0.6 0.0 copy-start
  0.6 1.3 %copy-done = bf16[768,768]{1,0:T(8,128)(2,1)S(1)} copy-done((bf16[768,768]{1,0:T(8,128)(2,1)S(1)}, bf16[768,768]{1,0:T(8,128)(2,1)}, u32[]{:S(2)}) %copy-start) | copy-done | bytes 1179672
  1.9 0.0 copy-start.3
  1.9 2.7 %convert_add_fusion = f32[768,768]{1,0:T(8,128)S(1)} fusion(bf16[768,768]{1,0:T(8,128)(2,1)S(1)} %copy-done, bf16[768,768]{1,0:T(8,128)(2,1)} %param.5, bf16[1,768,768]{2,1,0:T(8,128)(2,1)} %param.6), kind=kOutput, calls=%fused_computation | convolution fusion | flops 907149312 | bytes 5898240 | tf_op jit(solution)/shard_map/dot_general | solution.py:32
  4.7 0.0 copy-done.3
  4.7 2.0 %convolution_bitcast_fusion = f32[8,768]{1,0:T(8,128)S(1)} fusion(f32[768,768]{1,0:T(8,128)S(1)} %convert_add_fusion, f32[768,8]{0,1:T(8,128)S(1)} %copy-done.3), kind=kOutput, calls=%fused_computation.3 | convolution fusion | flops 56623104 | bytes 2408448 | tf_op jit(solution)/shard_map/dot_general | solution.py:36
  6.7 0.7 broadcast_in_dim.16
  7.4 1.6 %reshape.51 = f32[32,1,768]{2,1,0:T(1,128)} reshape(f32[4,8,768]{2,1,0:T(8,128)} %broadcast_in_dim.16) | data formatting | bytes 196608 | tf_op jit(solution)/shard_map/reshape | solution.py:22
  9.0 18.6 %all_to_all.30 = f32[32,1,768]{2,1,0:T(1,128)} all-to-all(f32[32,1,768]{2,1,0:T(1,128)} %reshape.51), channel_id=1, replica_groups=mesh['inner'=32,'outer'=16] {'inner'}, dimensions={0} | all-to-all | bytes 196608 | tf_op jit(solution)/shard_map/all_to_all | solution.py:15
  27.6 1.0 reduce_sum.36
  28.6 23.9 %all_to_all.31 = f32[16,1,768]{2,1,0:T(1,128)} all-to-all(f32[16,1,768]{2,1,0:T(1,128)S(1)} %broadcast_in_dim.17), channel_id=1, replica_groups=mesh['inner'=32,'outer'=16] {'outer'}, dimensions={0} | all-to-all | bytes 98304 | tf_op jit(solution)/shard_map/all_to_all | solution.py:15
  52.5 0.8 reduce_sum.37
  53.4 8.8 %all_to_all.32 = f32[8,1,768]{2,1,0:T(1,128)S(1)} all-to-all(f32[8,1,768]{2,1,0:T(1,128)S(1)} %broadcast_in_dim.18), channel_id=1, replica_groups={{0,16,32,48,64,80,96,112},{128,144,160,176,192,208,224,240},{256,272,28..., dimensions={0} | all-to-all | bytes 49152 | tf_op jit(solution)/shard_map/all_to_all | solution.py:15
  62.2 0.0 copy-start.2
  62.2 0.6 copy-done.2
  62.8 0.1 fusion.4
  62.9 0.1 copy.14
  63.0 0.7 cholesky.16
  63.7 0.1 select_reduce_fusion
  63.8 0.6 compare_reduce_fusion
  64.4 0.6 fusion.9
  65.1 0.6 custom-call.6
  65.7 1.0 fusion.2
  66.7 0.0 copy-start.1
  66.7 0.6 copy-done.1
  67.3 1.2 %fusion.12 = f32[8,768]{1,0:T(8,128)S(1)} fusion(f32[8,768]{1,0:T(8,128)S(1)} %fusion.2, f32[768,768]{1,0:T(8,128)S(1)} %convert_add_fusion), kind=kOutput, calls=%fused_computation.22 | convolution fusion | flops 56623104 | bytes 2408448 | tf_op jit(solution)/shard_map/dot_general | solution.py:40
  68.5 0.7 broadcast_in_dim.19
  69.2 1.6 %reshape.53 = f32[32,1,768]{2,1,0:T(1,128)} reshape(f32[4,8,768]{2,1,0:T(8,128)} %broadcast_in_dim.19) | data formatting | bytes 196608 | tf_op jit(solution)/shard_map/reshape | solution.py:22
  70.8 12.5 %all_to_all.33 = f32[32,1,768]{2,1,0:T(1,128)} all-to-all(f32[32,1,768]{2,1,0:T(1,128)} %reshape.53), channel_id=1, replica_groups=mesh['inner'=32,'outer'=16] {'inner'}, dimensions={0} | all-to-all | bytes 196608 | tf_op jit(solution)/shard_map/all_to_all | solution.py:15
  83.3 1.0 reduce_sum.38
  84.3 14.8 %all_to_all.34 = f32[16,1,768]{2,1,0:T(1,128)} all-to-all(f32[16,1,768]{2,1,0:T(1,128)S(1)} %broadcast_in_dim.20), channel_id=1, replica_groups=mesh['inner'=32,'outer'=16] {'outer'}, dimensions={0} | all-to-all | bytes 98304 | tf_op jit(solution)/shard_map/all_to_all | solution.py:15
  99.1 0.8 reduce_sum.39
  99.9 8.6 %all_to_all.35 = f32[8,1,768]{2,1,0:T(1,128)S(1)} all-to-all(f32[8,1,768]{2,1,0:T(1,128)S(1)} %broadcast_in_dim.21), channel_id=1, replica_groups={{0,16,32,48,64,80,96,112},{128,144,160,176,192,208,224,240},{256,272,28..., dimensions={0} | all-to-all | bytes 49152 | tf_op jit(solution)/shard_map/all_to_all | solution.py:15
  108.6 3.9 %fusion = bf16[1,768,768]{2,1,0:T(8,128)(2,1)} fusion(f32[768,768]{1,0:T(8,128)S(1)} %convert_add_fusion, f32[8,768]{1,0:T(8,128)} %copy-done.1, f32[8,1,768]{2,1,0:T(1,128)S(1)} %all_to_all.35), kind=kOutput, calls=%fused_computation.2 | convolution fusion | flops 58392576 | bytes 3588096 | tf_op jit(solution)/shard_map/dot_general | solution.py:42
  112.5 0.6 copy.34
  (5 shorter events, 0.1 us)
Async XLA Ops:
  0.6 1.3 %copy-start = (bf16[768,768]{1,0:T(8,128)(2,1)S(1)}, bf16[768,768]{1,0:T(8,128)(2,1)}, u32[]{:S(2)}) copy-start(bf16[768,768]{1,0:T(8,128)(2,1)} %param.4) | copy-start | bytes 3538948
  1.9 2.8 %copy-start.3 = (f32[768,8]{0,1:T(8,128)S(1)}, f32[768,8]{0,1:T(8,128)}, u32[]{:S(2)}) copy-start(f32[768,8]{0,1:T(8,128)} %param.7) | copy-start | bytes 73732
  62.2 0.6 copy-start.2
  66.7 0.6 copy-start.1

commit v2 on v0

v2 whole, which is shorter than its diff:
```python
import functools
import jax
import jax.numpy as jnp
from jax import lax
from jax.experimental import pallas as pl
from jax.experimental.pallas import tpu as pltpu
from jax.sharding import PartitionSpec as P

BLOCK = 256
LANES = 128
BF16 = jnp.bfloat16
F32 = jnp.float32
VMEM_BYTES = 24 * 1024 * 1024


def split(values, terms):
    found = []
    for at in range(terms):
        found.append(values.astype(BF16))
        if at + 1 < terms:
            values = values - found[-1].astype(F32)
    return found


def store_rows(parts_ref, rows, at, copies):
    rank = rows.shape[0]
    for tile in range(rows.shape[1] // LANES):
        piece = rows[:, tile * LANES:(tile + 1) * LANES]
        for copy in range(copies):
            parts_ref[copy * rank:(copy + 1) * rank, at + tile, :] = piece


def merge_kernel(a_hbm, g_hbm, e_hbm, q_hbm, hi_ref, lo_ref, parts_ref, a_buf, g_buf, e_buf, q_buf, sems):
    width, height = g_buf.shape[1], hi_ref.shape[0]
    blocks = height // BLOCK
    rank = q_buf.shape[0]
    copies = parts_ref.shape[0] // rank
    q_copy = pltpu.make_async_copy(q_hbm, q_buf, sems.at[1 + 2 * blocks])
    g_copy = pltpu.make_async_copy(g_hbm, g_buf, sems.at[0])
    a_copies, e_copies = [], []
    for b in range(blocks):
        at = pl.ds(b * BLOCK, BLOCK)
        a_copies.append(pltpu.make_async_copy(a_hbm.at[:, at], a_buf.at[b], sems.at[1 + b]))
        e_copies.append(pltpu.make_async_copy(e_hbm.at[at, :], e_buf.at[b], sems.at[1 + blocks + b]))
    a_copies[0].start()
    g_copy.start()
    q_copy.start()
    for b in range(blocks):
        if b > 0:
            a_copies[b].start()
        e_copies[b].start()
    q_copy.wait()
    q_terms = split(q_buf[...], 3)
    q_rows = jnp.concatenate(q_terms, axis=0)
    a_copies[0].wait()
    g_copy.wait()
    for b in range(blocks):
        if b > 0:
            a_copies[b].wait()
        gradient = lax.dot_general(
            a_buf[b], g_buf[...], (((0,), (0,)), ((), ())), preferred_element_type=F32
        )
        e_copies[b].wait()
        merged = gradient + e_buf[b].astype(F32)
        terms = split(merged, 3)
        at = slice(b * BLOCK, (b + 1) * BLOCK)
        hi_ref[at, :] = terms[0]
        lo_ref[at, :] = terms[1]
        total = jnp.zeros((rank, BLOCK), F32)
        for order, term in reversed(list(enumerate(terms))):
            used = (3 - order) * rank
            product = lax.dot_general(
                q_rows[:used], term, (((1,), (1,)), ((), ())), preferred_element_type=F32
            )
            for first in reversed(range(0, used, rank)):
                total = total + product[first:first + rank]
        store_rows(parts_ref, total, b * (BLOCK // LANES), copies)


def vmem(shape, dtype):
    return pltpu.VMEM(shape, dtype)


def in_vmem(x):
    return pltpu.with_memory_space_constraint(x, pltpu.VMEM)


def in_hbm(x):
    return pltpu.with_memory_space_constraint(x, pltpu.HBM)


SPEC_VMEM = pl.BlockSpec(memory_space=pltpu.VMEM)
SPEC_ANY = pl.BlockSpec(memory_space=pl.ANY)


def merge(activations, out_grads, error, q_rows, peers):
    tokens, height = activations.shape
    width = out_grads.shape[1]
    blocks = height // BLOCK
    return pl.pallas_call(
        merge_kernel,
        name="merge",
        out_shape=(
            vmem((height, width), BF16),
            vmem((height, width), BF16),
            vmem((peers, height // LANES, LANES), F32),
        ),
        in_specs=[SPEC_ANY] * 4,
        out_specs=(SPEC_VMEM,) * 3,
        scratch_shapes=[
            pltpu.VMEM((blocks, tokens, BLOCK), BF16),
            pltpu.VMEM((tokens, width), BF16),
            pltpu.VMEM((blocks, BLOCK, width), BF16),
            pltpu.VMEM(q_rows.shape, F32),
            pltpu.SemaphoreType.DMA((2 + 2 * blocks,)),
        ],
        compiler_params=pltpu.CompilerParams(vmem_limit_bytes=VMEM_BYTES),
    )(in_hbm(activations), in_hbm(out_grads), in_hbm(error), in_hbm(q_rows))


def sum_kernel(in_ref, out_ref):
    total = in_ref[0]
    for at in range(1, in_ref.shape[0]):
        total = total + in_ref[at]
    for at in range(out_ref.shape[0]):
        out_ref[at] = total


def sum_parts(parts, copies):
    return pl.pallas_call(
        sum_kernel,
        name="sum_parts",
        out_shape=vmem((copies,) + parts.shape[1:], F32),
        in_specs=[SPEC_VMEM],
        out_specs=SPEC_VMEM,
        compiler_params=pltpu.CompilerParams(vmem_limit_bytes=VMEM_BYTES),
    )(in_vmem(parts))


def load_rows(parts_ref):
    return jnp.concatenate([parts_ref[:, at, :] for at in range(parts_ref.shape[1])], axis=1)


def basis_kernel(p_ref, hi_ref, lo_ref, basis_ref, parts_ref):
    rank = p_ref.shape[0]
    copies = parts_ref.shape[0] // rank
    rows = load_rows(p_ref)
    gram = lax.dot_general(
        rows, rows, (((1,), (1,)), ((), ())),
        precision=lax.Precision.HIGHEST, preferred_element_type=F32,
    )
    index = lax.broadcasted_iota(jnp.int32, (rank, 1), 0)
    for step in range(rank):
        scale = lax.rsqrt(gram[step:step + 1, step:step + 1])
        gram_row = gram[step:step + 1, :] * scale
        row = rows[step:step + 1, :] * scale
        column = gram[:, step:step + 1] * scale
        below = index > step
        here = index == step
        gram = jnp.where(below, gram - column * gram_row, gram)
        rows = jnp.where(here, row, jnp.where(below, rows - column * row, rows))
    basis_ref[...] = rows
    terms = jnp.concatenate(split(rows, 3), axis=0)
    high = jnp.dot(terms, hi_ref[...], preferred_element_type=F32)
    low = jnp.dot(terms[:2 * rank], lo_ref[...], preferred_element_type=F32)
    total = low[rank:] + high[2 * rank:] + low[:rank] + high[rank:2 * rank] + high[:rank]
    store_rows(parts_ref, total, 0, copies)


def basis(p_parts, hi, lo, peers):
    rank, tiles, _ = p_parts.shape
    return pl.pallas_call(
        basis_kernel,
        name="basis",
        out_shape=(
            vmem((rank, tiles * LANES), F32),
            vmem((peers, hi.shape[1] // LANES, LANES), F32),
        ),
        in_specs=[SPEC_VMEM] * 3,
        out_specs=(SPEC_VMEM,) * 2,
        compiler_params=pltpu.CompilerParams(vmem_limit_bytes=VMEM_BYTES),
    )(in_vmem(p_parts), in_vmem(hi), in_vmem(lo))


def error_kernel(devices_all, q_ref, basis_ref, hi_ref, lo_ref, error_hbm, q_out_ref, basis_out_ref, buf, sems):
    blocks = buf.shape[0]
    rows = load_rows(q_ref)
    q_out_ref[...] = rows
    basis_out_ref[...] = basis_ref[...]
    b1, b2, b3 = split(basis_ref[...] / devices_all, 3)
    q1, q2, q3 = split(rows, 3)
    left = jnp.concatenate([b1, b1, b2, b1, b2, b3], axis=0)
    right = jnp.concatenate([q1, q2, q1, q3, q2, q1], axis=0)
    copies = []
    for b in range(blocks):
        at = slice(b * BLOCK, (b + 1) * BLOCK)
        correction = lax.dot_general(
            left[:, at], right, (((0,), (0,)), ((), ())), preferred_element_type=F32
        )
        merged = hi_ref[at, :].astype(F32) + lo_ref[at, :].astype(F32)
        buf[b] = (merged - correction).astype(BF16)
        copies.append(pltpu.make_async_copy(buf.at[b], error_hbm.at[0, pl.ds(b * BLOCK, BLOCK), :], sems.at[b]))
        copies[-1].start()
    for copy in copies:
        copy.wait()


def new_error(q_parts, basis_rows, hi, lo, devices_all):
    height, width = hi.shape
    rank = basis_rows.shape[0]
    blocks = height // BLOCK
    return pl.pallas_call(
        functools.partial(error_kernel, devices_all),
        name="new_error",
        out_shape=(
            jax.ShapeDtypeStruct((1, height, width), BF16),
            jax.ShapeDtypeStruct((rank, width), F32),
            jax.ShapeDtypeStruct((rank, height), F32),
        ),
        in_specs=[SPEC_VMEM] * 4,
        out_specs=(SPEC_ANY, SPEC_VMEM, SPEC_VMEM),
        scratch_shapes=[
            pltpu.VMEM((blocks, BLOCK, width), BF16),
            pltpu.SemaphoreType.DMA((blocks,)),
        ],
        compiler_params=pltpu.CompilerParams(vmem_limit_bytes=VMEM_BYTES),
    )(in_vmem(q_parts), in_vmem(basis_rows), in_vmem(hi), in_vmem(lo))


def exchange(parts, axis, groups=None):
    return lax.all_to_all(parts, axis, 0, 0, axis_index_groups=groups)


def reduce_all(parts, rank):
    n_inner, n_outer = lax.axis_size("inner"), lax.axis_size("outer")
    groups = [list(range(first, first + rank)) for first in range(0, n_inner, rank)]
    parts = sum_parts(exchange(parts, "inner"), n_outer)
    parts = sum_parts(exchange(parts, "outer"), rank)
    return exchange(parts, "inner", groups)


def local(activations, out_grads, error_in, q_init):
    n_inner, n_outer = lax.axis_size("inner"), lax.axis_size("outer")
    rank = q_init.shape[1]
    hi, lo, parts = merge(activations, out_grads, error_in[0], q_init.T, n_inner)
    basis_rows, parts = basis(reduce_all(parts, rank), hi, lo, n_inner)
    error_out, q_rows, p_rows = new_error(reduce_all(parts, rank), basis_rows, hi, lo, n_inner * n_outer)
    return (error_out, p_rows.T, q_rows.T)


def solution(mesh):
    placed = (
        P(("inner", "outer"), None),
        P(("inner", "outer"), None),
        P(("inner", "outer"), None, None),
        P(),
    )
    return jax.shard_map(
        local,
        mesh=mesh,
        in_specs=placed,
        out_specs=(P(("inner", "outer"), None, None), P(), P()),
        check_vma=False,
    )
```

time: 306 us -> 95.3 us (0.31)
  the two profiles are of different devices: /device:TPU:32 before, /device:TPU:1 now
where the time goes in v2:
time: 95.3 us; the launch traced here: 95 us
  blocking collectives  86.4 us (91%)
  Pallas kernels  7.95 us (8%)
    all_to_all x6, blocking collectives, exchange(): return lax.all_to_all(parts, axis, 0, 0, axis_index_groups=groups)  86.4 us
    pallas_call x1, Pallas kernels, merge(): pl.pallas_call(merge_kernel, name='merge', out_shape=(vmem((height, width...  4.58 us
    pallas_call x1, Pallas kernels, new_error(): pl.pallas_call(functools.partial(error_kernel, devices_all), name='new_er...  1.96 us

profile of v2, /device:TPU:1, one launch (start us, length us, event | category | flops | bytes accessed | tf_op | source)
XLA Modules:
  0.0 95.0 jit_solution(12713286571145919710)
XLA Ops:
  0.6 4.6 %merge.1 = (bf16[768,768]{1,0:T(8,128)(2,1)S(1)}, bf16[768,768]{1,0:T(8,128)(2,1)S(1)}, f32[32,6,128]{2,1,0:T(8,128)S(1)}) custom-call(bf16[768,768]{1,0:T(8,128)(2,1)} %a_hbm.1, bf16[768,768]{1,0:T(8,128)(2,1)} %g_hbm.1, bf16[768,768]{1,0:T(8,128)(2,1)} %bitcast.4, f32[8,768]{1,0:T(8,128)} %bitcast.5), custom_call_target="tpu_custom_call" | custom-call | tf_op jit(solution)/shard_map/merge/pallas_call | solution.py:100
  5.2 17.3 %all_to_all.30.in_ref = f32[32,6,128]{2,1,0:T(8,128)S(1)} all-to-all(f32[32,6,128]{2,1,0:T(8,128)S(1)} %get-tuple-element.11), channel_id=1, replica_groups=mesh['inner'=32,'outer'=16] {'inner'}, dimensions={0} | all-to-all | bytes 196608 | tf_op jit(solution)/shard_map/all_to_all | solution.py:231
  22.6 25.1 %all_to_all.31.in_ref = f32[16,6,128]{2,1,0:T(8,128)S(1)} all-to-all(f32[16,6,128]{2,1,0:T(8,128)S(1)} %sum_parts.4), channel_id=1, replica_groups=mesh['inner'=32,'outer'=16] {'outer'}, dimensions={0} | all-to-all | bytes 98304 | tf_op jit(solution)/shard_map/all_to_all | solution.py:231
  47.7 9.2 %all_to_all.32.p_ref = f32[8,6,128]{2,1,0:T(8,128)S(1)} all-to-all(f32[8,6,128]{2,1,0:T(8,128)S(1)} %sum_parts.5), channel_id=1, replica_groups={{0,16,32,48,64,80,96,112},{128,144,160,176,192,208,224,240},{256,272,28..., dimensions={0} | all-to-all | bytes 49152 | tf_op jit(solution)/shard_map/all_to_all | solution.py:231
  56.9 1.3 %basis.1 = (f32[8,768]{1,0:T(8,128)S(1)}, f32[32,6,128]{2,1,0:T(8,128)S(1)}) custom-call(f32[8,6,128]{2,1,0:T(8,128)S(1)} %all_to_all.32.p_ref, bf16[768,768]{1,0:T(8,128)(2,1)S(1)} %get-tuple-element.12.hi_ref, bf16[768,768]{1,0:T(8,128)(2,1)S(1)} %get-tuple-element.13.lo_ref), custom_call_target="tpu_custom_call" | custom-call | tf_op jit(solution)/shard_map/basis/pallas_call | solution.py:172
  58.2 11.5 %all_to_all.33.in_ref = f32[32,6,128]{2,1,0:T(8,128)S(1)} all-to-all(f32[32,6,128]{2,1,0:T(8,128)S(1)} %get-tuple-element.14), channel_id=1, replica_groups=mesh['inner'=32,'outer'=16] {'inner'}, dimensions={0} | all-to-all | bytes 196608 | tf_op jit(solution)/shard_map/all_to_all | solution.py:231
  69.7 14.3 %all_to_all.34.in_ref = f32[16,6,128]{2,1,0:T(8,128)S(1)} all-to-all(f32[16,6,128]{2,1,0:T(8,128)S(1)} %sum_parts.6), channel_id=1, replica_groups=mesh['inner'=32,'outer'=16] {'outer'}, dimensions={0} | all-to-all | bytes 98304 | tf_op jit(solution)/shard_map/all_to_all | solution.py:231
  84.1 8.9 %all_to_all.35.q_ref = f32[8,6,128]{2,1,0:T(8,128)S(1)} all-to-all(f32[8,6,128]{2,1,0:T(8,128)S(1)} %sum_parts.7), channel_id=1, replica_groups={{0,16,32,48,64,80,96,112},{128,144,160,176,192,208,224,240},{256,272,28..., dimensions={0} | all-to-all | bytes 49152 | tf_op jit(solution)/shard_map/all_to_all | solution.py:231
  93.0 2.0 %new_error.1 = (bf16[1,768,768]{2,1,0:T(8,128)(2,1)}, f32[8,768]{1,0:T(8,128)}, f32[8,768]{1,0:T(8,128)}) custom-call(f32[8,6,128]{2,1,0:T(8,128)S(1)} %all_to_all.35.q_ref, f32[8,768]{1,0:T(8,128)S(1)} %get-tuple-element.15.basis_ref, bf16[768,768]{1,0:T(8,128)(2,1)S(1)} %get-tuple-element.12.hi_ref, bf16[768,768]{1,0:T(8,128)(2,1)S(1)} %get-tuple-element.13.lo_ref), custom_call_target="tpu_custom_call" | custom-call | tf_op jit(solution)/shard_map/new_error/pallas_call | solution.py:212
  (4 shorter events, 0.1 us)

commit v3 on v0

v3 whole, which is shorter than its diff:
```python
import functools
import jax
import jax.numpy as jnp
from jax import lax
from jax.experimental import pallas as pl
from jax.experimental.pallas import tpu as pltpu
from jax.sharding import PartitionSpec as P

BF16 = jnp.bfloat16
F32 = jnp.float32
TERMS = 3
VMEM_BYTES = 24 * 1024 * 1024
SPEC_VMEM = pl.BlockSpec(memory_space=pltpu.VMEM)
SPEC_ANY = pl.BlockSpec(memory_space=pl.ANY)
PARAMS = pltpu.CompilerParams(vmem_limit_bytes=VMEM_BYTES)


def in_hbm(x):
    return pltpu.with_memory_space_constraint(x, pltpu.HBM)


def in_vmem(x):
    return pltpu.with_memory_space_constraint(x, pltpu.VMEM)


def split(values):
    found = []
    for at in range(TERMS):
        found.append(values.astype(BF16))
        values = values - found[-1].astype(F32)
    return found


def stack(values):
    return jnp.concatenate(split(values), axis=0)


def unstack(product):
    rank = product.shape[0] // TERMS
    return product[2 * rank:] + product[rank:2 * rank] + product[:rank]


def dot_nn(left, right):
    return lax.dot_general(left, right, (((1,), (0,)), ((), ())), preferred_element_type=F32)


def dot_nt(left, right):
    return lax.dot_general(left, right, (((1,), (1,)), ((), ())), preferred_element_type=F32)


def dot_tn(left, right):
    return lax.dot_general(left, right, (((0,), (0,)), ((), ())), preferred_element_type=F32)


def store_parts(parts_ref, rows):
    for at in range(rows.shape[0]):
        parts_ref[at] = rows[at:at + 1]


def sum_rows(parts_ref, rank):
    rows = []
    for at in range(rank):
        row = parts_ref[at]
        for other in range(at + rank, parts_ref.shape[0], rank):
            row = row + parts_ref[other]
        rows.append(row)
    return jnp.concatenate(rows, axis=0)


def left_kernel(a_hbm, g_hbm, e_hbm, q_hbm, a_ref, g_ref, e_ref, parts_ref, q_buf, sems):
    pairs = ((q_hbm, q_buf), (g_hbm, g_ref), (e_hbm, e_ref), (a_hbm, a_ref))
    copies = [pltpu.make_async_copy(*pair, sems.at[at]) for at, pair in enumerate(pairs)]
    for copy in copies:
        copy.start()
    q_copy, g_copy, e_copy, a_copy = copies
    q_copy.wait()
    terms = stack(q_buf[...])
    g_copy.wait()
    tokens = stack(unstack(dot_nt(terms, g_ref[...])))
    e_copy.wait()
    from_error = unstack(dot_nt(terms, e_ref[...]))
    a_copy.wait()
    store_parts(parts_ref, unstack(dot_nn(tokens, a_ref[...])) + from_error)


def left_term(activations, out_grads, error, q_rows):
    rank, width = q_rows.shape
    height = activations.shape[1]
    return pl.pallas_call(
        left_kernel,
        name="left_term",
        out_shape=(
            pltpu.VMEM(activations.shape, BF16),
            pltpu.VMEM(out_grads.shape, BF16),
            pltpu.VMEM(error.shape, BF16),
            pltpu.VMEM((rank, 1, height), F32),
        ),
        in_specs=[SPEC_ANY] * 4,
        out_specs=(SPEC_VMEM,) * 4,
        scratch_shapes=[pltpu.VMEM(q_rows.shape, F32), pltpu.SemaphoreType.DMA((4,))],
        compiler_params=PARAMS,
    )(in_hbm(activations), in_hbm(out_grads), in_hbm(error), in_hbm(q_rows))


def sum_kernel(in_ref, out_ref):
    total = in_ref[0]
    for at in range(1, in_ref.shape[0]):
        total = total + in_ref[at]
    for at in range(out_ref.shape[0]):
        out_ref[at] = total


def sum_parts(parts, copies):
    return pl.pallas_call(
        sum_kernel,
        name="sum_parts",
        out_shape=pltpu.VMEM((copies,) + parts.shape[1:], F32),
        in_specs=[SPEC_VMEM],
        out_specs=SPEC_VMEM,
        compiler_params=PARAMS,
    )(in_vmem(parts))


def inverse_factor(rows):
    rank = rows.shape[0]
    gram = lax.dot_general(
        rows, rows, (((1,), (1,)), ((), ())),
        precision=lax.Precision.HIGHEST, preferred_element_type=F32,
    )
    index = lax.broadcasted_iota(jnp.int32, (rank, 1), 0)
    inverse = (index == lax.broadcasted_iota(jnp.int32, (rank, rank), 1)).astype(F32)
    for step in range(rank):
        at = slice(step, step + 1)
        scale = lax.rsqrt(gram[at, at])
        column = jnp.where(index > step, gram[:, at] * scale, 0.0)
        gram = gram - column * (gram[at, :] * scale)
        row = inverse[at, :] * scale
        inverse = jnp.where(index == step, row, inverse - column * row)
    return inverse


def combine(factors, rows):
    total = factors[:, 0:1] * rows[0:1, :]
    for at in range(1, rows.shape[0]):
        total = total + factors[:, at:at + 1] * rows[at:at + 1, :]
    return total


def right_kernel(p_ref, a_ref, g_ref, e_ref, basis_ref, parts_ref):
    rank = parts_ref.shape[0]
    rows = sum_rows(p_ref, rank)
    inverse = inverse_factor(rows)
    basis_ref[...] = combine(inverse, rows)
    terms = stack(rows)
    tokens = stack(unstack(dot_nt(terms, a_ref[...])))
    products = unstack(dot_nn(tokens, g_ref[...])) + unstack(dot_nn(terms, e_ref[...]))
    store_parts(parts_ref, combine(inverse, products))


def right_term(p_parts, activations, out_grads, error, rank):
    return pl.pallas_call(
        right_kernel,
        name="right_term",
        out_shape=(
            pltpu.VMEM((rank, activations.shape[1]), F32),
            pltpu.VMEM((rank, 1, out_grads.shape[1]), F32),
        ),
        in_specs=[SPEC_VMEM] * 4,
        out_specs=(SPEC_VMEM,) * 2,
        compiler_params=PARAMS,
    )(in_vmem(p_parts), in_vmem(activations), in_vmem(out_grads), in_vmem(error))


def error_kernel(devices_all, q_ref, basis_ref, a_ref, g_ref, e_ref, error_hbm, q_hbm, basis_hbm, buf, q_buf, sems):
    basis_copy = pltpu.make_async_copy(basis_ref, basis_hbm, sems.at[0])
    basis_copy.start()
    rows = sum_rows(q_ref, basis_ref.shape[0])
    q_buf[...] = rows
    q_copy = pltpu.make_async_copy(q_buf, q_hbm, sems.at[1])
    q_copy.start()
    b1, b2, b3 = split(basis_ref[...] / -devices_all)
    q1, q2, q3 = split(rows)
    left = jnp.concatenate([b1, b1, b2, b1, b2, b3], axis=0)
    right = jnp.concatenate([q1, q2, q1, q3, q2, q1], axis=0)
    merged = dot_tn(a_ref[...], g_ref[...]) + e_ref[...].astype(F32)
    buf[0] = (merged + dot_tn(left, right)).astype(BF16)
    error_copy = pltpu.make_async_copy(buf, error_hbm, sems.at[2])
    error_copy.start()
    basis_copy.wait()
    q_copy.wait()
    error_copy.wait()


def new_error(q_parts, basis_rows, activations, out_grads, error, devices_all):
    height, width = error.shape
    rank = basis_rows.shape[0]
    return pl.pallas_call(
        functools.partial(error_kernel, devices_all),
        name="new_error",
        out_shape=(
            jax.ShapeDtypeStruct((1, height, width), BF16),
            jax.ShapeDtypeStruct((rank, width), F32),
            jax.ShapeDtypeStruct((rank, height), F32),
        ),
        in_specs=[SPEC_VMEM] * 5,
        out_specs=(SPEC_ANY,) * 3,
        scratch_shapes=[
            pltpu.VMEM((1, height, width), BF16),
            pltpu.VMEM((rank, width), F32),
            pltpu.SemaphoreType.DMA((3,)),
        ],
        compiler_params=PARAMS,
    )(*[in_vmem(x) for x in (q_parts, basis_rows, activations, out_grads, error)])


def exchange(parts, axis, groups=None):
    return lax.all_to_all(parts, axis, 0, 0, axis_index_groups=groups)


def reduce_all(parts):
    rank = parts.shape[0]
    n_inner, n_outer = lax.axis_size("inner"), lax.axis_size("outer")
    groups = [list(range(first, first + rank)) for first in range(0, n_inner, rank)]
    parts = sum_parts(exchange(parts, "inner", groups), n_outer)
    parts = sum_parts(exchange(parts, "outer"), n_inner)
    return exchange(parts, "inner")


def local(activations, out_grads, error_in, q_init):
    devices_all = lax.axis_size("inner") * lax.axis_size("outer")
    *operands, parts = left_term(activations, out_grads, error_in[0], q_init.T)
    basis_rows, parts = right_term(reduce_all(parts), *operands, q_init.shape[1])
    error_out, q_rows, p_rows = new_error(reduce_all(parts), basis_rows, *operands, devices_all)
    return (error_out, p_rows.T, q_rows.T)


def solution(mesh):
    placed = (
        P(("inner", "outer"), None),
        P(("inner", "outer"), None),
        P(("inner", "outer"), None, None),
        P(),
    )
    return jax.shard_map(
        local,
        mesh=mesh,
        in_specs=placed,
        out_specs=(P(("inner", "outer"), None, None), P(), P()),
        check_vma=False,
    )
```

time: 306 us -> 92.2 us (0.30)
  the two profiles are of different devices: /device:TPU:32 before, /device:TPU:1 now
where the time goes in v3:
time: 92.2 us; the launch traced here: 91.9 us
  blocking collectives  85 us (92%)
  Pallas kernels  6.28 us (7%)
    all_to_all x6, blocking collectives, exchange(): return lax.all_to_all(parts, axis, 0, 0, axis_index_groups=groups)  85 us
    pallas_call x1, Pallas kernels, left_term(): pl.pallas_call(left_kernel, name='left_term', out_shape=(pltpu.VMEM(activ...  2.73 us
    pallas_call x1, Pallas kernels, new_error(): pl.pallas_call(functools.partial(error_kernel, devices_all), name='new_er...  2.48 us

profile of v3, /device:TPU:1, one launch (start us, length us, event | category | flops | bytes accessed | tf_op | source)
XLA Modules:
  0.0 91.9 jit_solution(18271452020108377247)
XLA Ops:
  0.6 2.7 %left_term.1 = (bf16[768,768]{1,0:T(8,128)(2,1)S(1)}, bf16[768,768]{1,0:T(8,128)(2,1)S(1)}, bf16[768,768]{1,0:T(8,128)(2,1)S(1)}, f32[8,1,768]{2,1,0:T(1,128)S(1)}) custom-call(bf16[768,768]{1,0:T(8,128)(2,1)} %a_hbm.1, bf16[768,768]{1,0:T(8,128)(2,1)} %g_hbm.1, bf16[768,768]{1,0:T(8,128)(2,1)} %bitcast.4, f32[8,768]{1,0:T(8,128)} %bitcast.5), custom_call_target="tpu_custom_call" | custom-call | tf_op jit(solution)/shard_map/left_term/pallas_call | solution.py:89
  3.4 13.9 %all_to_all.30.in_ref = f32[8,1,768]{2,1,0:T(1,128)S(1)} all-to-all(f32[8,1,768]{2,1,0:T(1,128)S(1)} %get-tuple-element.12), channel_id=1, replica_groups={{0,16,32,48,64,80,96,112},{128,144,160,176,192,208,224,240},{256,272,28..., dimensions={0} | all-to-all | bytes 49152 | tf_op jit(solution)/shard_map/all_to_all | solution.py:217
  17.3 22.8 %all_to_all.31.in_ref = f32[16,1,768]{2,1,0:T(1,128)S(1)} all-to-all(f32[16,1,768]{2,1,0:T(1,128)S(1)} %sum_parts.4), channel_id=1, replica_groups=mesh['inner'=32,'outer'=16] {'outer'}, dimensions={0} | all-to-all | bytes 98304 | tf_op jit(solution)/shard_map/all_to_all | solution.py:217
  40.1 14.4 %all_to_all.32.p_ref = f32[32,1,768]{2,1,0:T(1,128)S(1)} all-to-all(f32[32,1,768]{2,1,0:T(1,128)S(1)} %sum_parts.5), channel_id=1, replica_groups=mesh['inner'=32,'outer'=16] {'inner'}, dimensions={0} | all-to-all | bytes 196608 | tf_op jit(solution)/shard_map/all_to_all | solution.py:217
  54.5 1.0 %right_term.1 = (f32[8,768]{1,0:T(8,128)S(1)}, f32[8,1,768]{2,1,0:T(1,128)S(1)}) custom-call(f32[32,1,768]{2,1,0:T(1,128)S(1)} %all_to_all.32.p_ref, bf16[768,768]{1,0:T(8,128)(2,1)S(1)} %get-tuple-element.13.a_ref, bf16[768,768]{1,0:T(8,128)(2,1)S(1)} %get-tuple-element.14.g_ref, bf16[768,768]{1,0:T(8,128)(2,1)S(1)} %get-tuple-element.15.e_ref), custom_call_target="tpu_custom_call" | custom-call | tf_op jit(solution)/shard_map/right_term/pallas_call | solution.py:161
  55.5 7.4 %all_to_all.33.in_ref = f32[8,1,768]{2,1,0:T(1,128)S(1)} all-to-all(f32[8,1,768]{2,1,0:T(1,128)S(1)} %get-tuple-element.16), channel_id=1, replica_groups={{0,16,32,48,64,80,96,112},{128,144,160,176,192,208,224,240},{256,272,28..., dimensions={0} | all-to-all | bytes 49152 | tf_op jit(solution)/shard_map/all_to_all | solution.py:217
  63.0 14.0 %all_to_all.34.in_ref = f32[16,1,768]{2,1,0:T(1,128)S(1)} all-to-all(f32[16,1,768]{2,1,0:T(1,128)S(1)} %sum_parts.6), channel_id=1, replica_groups=mesh['inner'=32,'outer'=16] {'outer'}, dimensions={0} | all-to-all | bytes 98304 | tf_op jit(solution)/shard_map/all_to_all | solution.py:217
  77.0 12.4 %all_to_all.35.q_ref = f32[32,1,768]{2,1,0:T(1,128)S(1)} all-to-all(f32[32,1,768]{2,1,0:T(1,128)S(1)} %sum_parts.7), channel_id=1, replica_groups=mesh['inner'=32,'outer'=16] {'inner'}, dimensions={0} | all-to-all | bytes 196608 | tf_op jit(solution)/shard_map/all_to_all | solution.py:217
  89.5 2.5 %new_error.1 = (bf16[1,768,768]{2,1,0:T(8,128)(2,1)}, f32[8,768]{1,0:T(8,128)}, f32[8,768]{1,0:T(8,128)}) custom-call(f32[32,1,768]{2,1,0:T(1,128)S(1)} %all_to_all.35.q_ref, f32[8,768]{1,0:T(8,128)S(1)} %get-tuple-element.17.basis_ref, bf16[768,768]{1,0:T(8,128)(2,1)S(1)} %get-tuple-element.13.a_ref, bf16[768,768]{1,0:T(8,128)(2,1)S(1)} %get-tuple-element.14.g_ref, ...), custom_call_target="tpu_custom_call" | custom-call | tf_op jit(solution)/shard_map/new_error/pallas_call | solution.py:197
  (4 shorter events, 0.1 us)

commit v4 on v3

--- a/solution.py
+++ b/solution.py
@@ -67,7 +67,12 @@
     return jnp.concatenate(rows, axis=0)
 
 
-def left_kernel(a_hbm, g_hbm, e_hbm, q_hbm, a_ref, g_ref, e_ref, parts_ref, q_buf, sems):
+def has_time(n_outer):
+    at = lax.axis_index("outer")
+    return (at <= n_outer // 4) | (at >= n_outer - n_outer // 4)
+
+
+def left_kernel(n_outer, a_hbm, g_hbm, e_hbm, q_hbm, a_ref, g_ref, e_ref, merged_ref, parts_ref, q_buf, sems):
     pairs = ((q_hbm, q_buf), (g_hbm, g_ref), (e_hbm, e_ref), (a_hbm, a_ref))
     copies = [pltpu.make_async_copy(*pair, sems.at[at]) for at, pair in enumerate(pairs)]
     for copy in copies:
@@ -82,21 +87,26 @@
     a_copy.wait()
     store_parts(parts_ref, unstack(dot_nn(tokens, a_ref[...])) + from_error)
 
-
-def left_term(activations, out_grads, error, q_rows):
+    @pl.when(has_time(n_outer))
+    def _():
+        merged_ref[...] = dot_tn(a_ref[...], g_ref[...]) + e_ref[...].astype(F32)
+
+
+def left_term(activations, out_grads, error, q_rows, n_outer):
     rank, width = q_rows.shape
     height = activations.shape[1]
     return pl.pallas_call(
-        left_kernel,
+        functools.partial(left_kernel, n_outer),
         name="left_term",
         out_shape=(
             pltpu.VMEM(activations.shape, BF16),
             pltpu.VMEM(out_grads.shape, BF16),
             pltpu.VMEM(error.shape, BF16),
+            pltpu.VMEM(error.shape, F32),
             pltpu.VMEM((rank, 1, height), F32),
         ),
         in_specs=[SPEC_ANY] * 4,
-        out_specs=(SPEC_VMEM,) * 4,
+        out_specs=(SPEC_VMEM,) * 5,
         scratch_shapes=[pltpu.VMEM(q_rows.shape, F32), pltpu.SemaphoreType.DMA((4,))],
         compiler_params=PARAMS,
     )(in_hbm(activations), in_hbm(out_grads), in_hbm(error), in_hbm(q_rows))
@@ -171,7 +181,10 @@
     )(in_vmem(p_parts), in_vmem(activations), in_vmem(out_grads), in_vmem(error))
 
 
-def error_kernel(devices_all, q_ref, basis_ref, a_ref, g_ref, e_ref, error_hbm, q_hbm, basis_hbm, buf, q_buf, sems):
+def error_kernel(
+    n_outer, devices_all, q_ref, basis_ref, a_ref, g_ref, e_ref, merged_ref,
+    error_hbm, q_hbm, basis_hbm, buf, q_buf, sems,
+):
     basis_copy = pltpu.make_async_copy(basis_ref, basis_hbm, sems.at[0])
     basis_copy.start()
     rows = sum_rows(q_ref, basis_ref.shape[0])
@@ -182,8 +195,17 @@
     q1, q2, q3 = split(rows)
     left = jnp.concatenate([b1, b1, b2, b1, b2, b3], axis=0)
     right = jnp.concatenate([q1, q2, q1, q3, q2, q1], axis=0)
-    merged = dot_tn(a_ref[...], g_ref[...]) + e_ref[...].astype(F32)
-    buf[0] = (merged + dot_tn(left, right)).astype(BF16)
+    early = has_time(n_outer)
+
+    @pl.when(early)
+    def _():
+        buf[0] = (merged_ref[...] + dot_tn(left, right)).astype(BF16)
+
+    @pl.when(jnp.logical_not(early))
+    def _():
+        merged = dot_tn(a_ref[...], g_ref[...]) + e_ref[...].astype(F32)
+        buf[0] = (merged + dot_tn(left, right)).astype(BF16)
+
     error_copy = pltpu.make_async_copy(buf, error_hbm, sems.at[2])
     error_copy.start()
     basis_copy.wait()
@@ -191,18 +213,18 @@
     error_copy.wait()
 
 
-def new_error(q_parts, basis_rows, activations, out_grads, error, devices_all):
+def new_error(q_parts, basis_rows, activations, out_grads, error, merged, n_outer, devices_all):
     height, width = error.shape
     rank = basis_rows.shape[0]
     return pl.pallas_call(
-        functools.partial(error_kernel, devices_all),
+        functools.partial(error_kernel, n_outer, devices_all),
         name="new_error",
         out_shape=(
             jax.ShapeDtypeStruct((1, height, width), BF16),
             jax.ShapeDtypeStruct((rank, width), F32),
             jax.ShapeDtypeStruct((rank, height), F32),
         ),
-        in_specs=[SPEC_VMEM] * 5,
+        in_specs=[SPEC_VMEM] * 6,
         out_specs=(SPEC_ANY,) * 3,
         scratch_shapes=[
             pltpu.VMEM((1, height, width), BF16),
@@ -210,7 +232,7 @@
             pltpu.SemaphoreType.DMA((3,)),
         ],
         compiler_params=PARAMS,
-    )(*[in_vmem(x) for x in (q_parts, basis_rows, activations, out_grads, error)])
+    )(*[in_vmem(x) for x in (q_parts, basis_rows, activations, out_grads, error, merged)])
 
 
 def exchange(parts, axis, groups=None):
@@ -227,10 +249,11 @@
 
 
 def local(activations, out_grads, error_in, q_init):
-    devices_all = lax.axis_size("inner") * lax.axis_size("outer")
-    *operands, parts = left_term(activations, out_grads, error_in[0], q_init.T)
+    n_outer = lax.axis_size("outer")
+    devices_all = lax.axis_size("inner") * n_outer
+    *operands, merged, parts = left_term(activations, out_grads, error_in[0], q_init.T, n_outer)
     basis_rows, parts = right_term(reduce_all(parts), *operands, q_init.shape[1])
-    error_out, q_rows, p_rows = new_error(reduce_all(parts), basis_rows, *operands, devices_all)
+    error_out, q_rows, p_rows = new_error(reduce_all(parts), basis_rows, *operands, merged, n_outer, devices_all)
     return (error_out, p_rows.T, q_rows.T)
 
 

time: 92.2 us -> 91.4 us (level)
  blocking collectives: 85 us -> 83.9 us
    all_to_all x6, blocking collectives: 85 us -> 83.9 us  [exchange(): return lax.all_to_all(parts, axis, 0, 0, axis_index_groups=groups)]
where the time goes in v4:
time: 91.4 us; the launch traced here: 91 us
  blocking collectives  83.9 us (92%)
  Pallas kernels  6.52 us (7%)
    all_to_all x6, blocking collectives, exchange(): return lax.all_to_all(parts, axis, 0, 0, axis_index_groups=groups)  83.9 us
    pallas_call x1, Pallas kernels, left_term(): pl.pallas_call(functools.partial(left_kernel, n_outer), name='left_term',...  3.87 us

profile of v4, /device:TPU:1, one launch (start us, length us, event | category | flops | bytes accessed | tf_op | source)
XLA Modules:
  0.0 91.0 jit_solution(14706564717310624147)
XLA Ops:
  0.6 3.9 %left_term.1 = (bf16[768,768]{1,0:T(8,128)(2,1)S(1)}, bf16[768,768]{1,0:T(8,128)(2,1)S(1)}, bf16[768,768]{1,0:T(8,128)(2,1)S(1)}, f32[768,768]{1,0:T(8,128)S(1)}, f32[8,1,768]{2,1,0:T(1,128)S(1)}) custom-call(bf16[768,768]{1,0:T(8,128)(2,1)} %a_hbm.1, bf16[768,768]{1,0:T(8,128)(2,1)} %g_hbm.1, bf16[768,768]{1,0:T(8,128)(2,1)} %bitcast.4, f32[8,768]{1,0:T(8,128)} %bitcast.5), custom_call_target="tpu_custom_call" | custom-call | tf_op jit(solution)/shard_map/left_term/pallas_call | solution.py:98
  4.5 13.9 %all_to_all.30.in_ref = f32[8,1,768]{2,1,0:T(1,128)S(1)} all-to-all(f32[8,1,768]{2,1,0:T(1,128)S(1)} %get-tuple-element.13), channel_id=1, replica_groups={{0,16,32,48,64,80,96,112},{128,144,160,176,192,208,224,240},{256,272,28..., dimensions={0} | all-to-all | bytes 49152 | tf_op jit(solution)/shard_map/all_to_all | solution.py:239
  18.4 21.7 %all_to_all.31.in_ref = f32[16,1,768]{2,1,0:T(1,128)S(1)} all-to-all(f32[16,1,768]{2,1,0:T(1,128)S(1)} %sum_parts.4), channel_id=1, replica_groups=mesh['inner'=32,'outer'=16] {'outer'}, dimensions={0} | all-to-all | bytes 98304 | tf_op jit(solution)/shard_map/all_to_all | solution.py:239
  40.1 14.4 %all_to_all.32.p_ref = f32[32,1,768]{2,1,0:T(1,128)S(1)} all-to-all(f32[32,1,768]{2,1,0:T(1,128)S(1)} %sum_parts.5), channel_id=1, replica_groups=mesh['inner'=32,'outer'=16] {'inner'}, dimensions={0} | all-to-all | bytes 196608 | tf_op jit(solution)/shard_map/all_to_all | solution.py:239
  54.5 1.0 %right_term.1 = (f32[8,768]{1,0:T(8,128)S(1)}, f32[8,1,768]{2,1,0:T(1,128)S(1)}) custom-call(f32[32,1,768]{2,1,0:T(1,128)S(1)} %all_to_all.32.p_ref, bf16[768,768]{1,0:T(8,128)(2,1)S(1)} %get-tuple-element.14.a_ref, bf16[768,768]{1,0:T(8,128)(2,1)S(1)} %get-tuple-element.15.g_ref, bf16[768,768]{1,0:T(8,128)(2,1)S(1)} %get-tuple-element.16.e_ref), custom_call_target="tpu_custom_call" | custom-call | tf_op jit(solution)/shard_map/right_term/pallas_call | solution.py:171
  55.5 7.4 %all_to_all.33.in_ref = f32[8,1,768]{2,1,0:T(1,128)S(1)} all-to-all(f32[8,1,768]{2,1,0:T(1,128)S(1)} %get-tuple-element.17), channel_id=1, replica_groups={{0,16,32,48,64,80,96,112},{128,144,160,176,192,208,224,240},{256,272,28..., dimensions={0} | all-to-all | bytes 49152 | tf_op jit(solution)/shard_map/all_to_all | solution.py:239
  63.0 14.0 %all_to_all.34.in_ref = f32[16,1,768]{2,1,0:T(1,128)S(1)} all-to-all(f32[16,1,768]{2,1,0:T(1,128)S(1)} %sum_parts.6), channel_id=1, replica_groups=mesh['inner'=32,'outer'=16] {'outer'}, dimensions={0} | all-to-all | bytes 98304 | tf_op jit(solution)/shard_map/all_to_all | solution.py:239
  77.0 12.4 %all_to_all.35.q_ref = f32[32,1,768]{2,1,0:T(1,128)S(1)} all-to-all(f32[32,1,768]{2,1,0:T(1,128)S(1)} %sum_parts.7), channel_id=1, replica_groups=mesh['inner'=32,'outer'=16] {'inner'}, dimensions={0} | all-to-all | bytes 196608 | tf_op jit(solution)/shard_map/all_to_all | solution.py:239
  89.5 1.6 %new_error.1 = (bf16[1,768,768]{2,1,0:T(8,128)(2,1)}, f32[8,768]{1,0:T(8,128)}, f32[8,768]{1,0:T(8,128)}) custom-call(f32[32,1,768]{2,1,0:T(1,128)S(1)} %all_to_all.35.q_ref, f32[8,768]{1,0:T(8,128)S(1)} %get-tuple-element.18.basis_ref, bf16[768,768]{1,0:T(8,128)(2,1)S(1)} %get-tuple-element.14.a_ref, bf16[768,768]{1,0:T(8,128)(2,1)S(1)} %get-tuple-element.15.g_ref, ...), custom_call_target="tpu_custom_call" | custom-call | tf_op jit(solution)/shard_map/new_error/pallas_call | solution.py:219
  (4 shorter events, 0.1 us)

commit v5 on v4

--- a/solution.py
+++ b/solution.py
@@ -6,6 +6,7 @@
 from jax.experimental.pallas import tpu as pltpu
 from jax.sharding import PartitionSpec as P
 
+BLOCK = 256
 BF16 = jnp.bfloat16
 F32 = jnp.float32
 TERMS = 3
@@ -199,18 +200,29 @@
 
     @pl.when(early)
     def _():
-        buf[0] = (merged_ref[...] + dot_tn(left, right)).astype(BF16)
+        height = buf.shape[1]
+        copies = []
+        for first in range(0, height, BLOCK):
+            at = slice(first, first + BLOCK)
+            buf[0, at, :] = (merged_ref[at, :] + dot_tn(left[:, at], right)).astype(BF16)
+            rows_at = pl.ds(first, BLOCK)
+            copies.append(pltpu.make_async_copy(
+                buf.at[:, rows_at], error_hbm.at[:, rows_at], sems.at[2 + first // BLOCK]
+            ))
+            copies[-1].start()
+        for copy in copies:
+            copy.wait()
 
     @pl.when(jnp.logical_not(early))
     def _():
         merged = dot_tn(a_ref[...], g_ref[...]) + e_ref[...].astype(F32)
         buf[0] = (merged + dot_tn(left, right)).astype(BF16)
-
-    error_copy = pltpu.make_async_copy(buf, error_hbm, sems.at[2])
-    error_copy.start()
+        copy = pltpu.make_async_copy(buf, error_hbm, sems.at[2])
+        copy.start()
+        copy.wait()
+
     basis_copy.wait()
     q_copy.wait()
-    error_copy.wait()
 
 
 def new_error(q_parts, basis_rows, activations, out_grads, error, merged, n_outer, devices_all):
@@ -229,7 +241,7 @@
         scratch_shapes=[
             pltpu.VMEM((1, height, width), BF16),
             pltpu.VMEM((rank, width), F32),
-            pltpu.SemaphoreType.DMA((3,)),
+            pltpu.SemaphoreType.DMA((2 + height // BLOCK,)),
         ],
         compiler_params=PARAMS,
     )(*[in_vmem(x) for x in (q_parts, basis_rows, activations, out_grads, error, merged)])

time: 91.4 us -> 91.2 us (level)
  no operation moved by 1% of the time
where the time goes in v5:
time: 91.2 us; the launch traced here: 90.8 us
  blocking collectives  83.9 us (92%)
  Pallas kernels  6.33 us (7%)
    all_to_all x6, blocking collectives, exchange(): return lax.all_to_all(parts, axis, 0, 0, axis_index_groups=groups)  83.9 us
    pallas_call x1, Pallas kernels, left_term(): pl.pallas_call(functools.partial(left_kernel, n_outer), name='left_term',...  3.87 us

profile of v5, /device:TPU:1, one launch (start us, length us, event | category | flops | bytes accessed | tf_op | source)
XLA Modules:
  0.0 90.8 jit_solution(15720195052302093514)
XLA Ops:
  0.6 3.9 %left_term.1 = (bf16[768,768]{1,0:T(8,128)(2,1)S(1)}, bf16[768,768]{1,0:T(8,128)(2,1)S(1)}, bf16[768,768]{1,0:T(8,128)(2,1)S(1)}, f32[768,768]{1,0:T(8,128)S(1)}, f32[8,1,768]{2,1,0:T(1,128)S(1)}) custom-call(bf16[768,768]{1,0:T(8,128)(2,1)} %a_hbm.1, bf16[768,768]{1,0:T(8,128)(2,1)} %g_hbm.1, bf16[768,768]{1,0:T(8,128)(2,1)} %bitcast.4, f32[8,768]{1,0:T(8,128)} %bitcast.5), custom_call_target="tpu_custom_call" | custom-call | tf_op jit(solution)/shard_map/left_term/pallas_call | solution.py:99
  4.5 13.9 %all_to_all.30.in_ref = f32[8,1,768]{2,1,0:T(1,128)S(1)} all-to-all(f32[8,1,768]{2,1,0:T(1,128)S(1)} %get-tuple-element.13), channel_id=1, replica_groups={{0,16,32,48,64,80,96,112},{128,144,160,176,192,208,224,240},{256,272,28..., dimensions={0} | all-to-all | bytes 49152 | tf_op jit(solution)/shard_map/all_to_all | solution.py:251
  18.4 21.7 %all_to_all.31.in_ref = f32[16,1,768]{2,1,0:T(1,128)S(1)} all-to-all(f32[16,1,768]{2,1,0:T(1,128)S(1)} %sum_parts.4), channel_id=1, replica_groups=mesh['inner'=32,'outer'=16] {'outer'}, dimensions={0} | all-to-all | bytes 98304 | tf_op jit(solution)/shard_map/all_to_all | solution.py:251
  40.1 14.4 %all_to_all.32.p_ref = f32[32,1,768]{2,1,0:T(1,128)S(1)} all-to-all(f32[32,1,768]{2,1,0:T(1,128)S(1)} %sum_parts.5), channel_id=1, replica_groups=mesh['inner'=32,'outer'=16] {'inner'}, dimensions={0} | all-to-all | bytes 196608 | tf_op jit(solution)/shard_map/all_to_all | solution.py:251
  54.5 1.0 %right_term.1 = (f32[8,768]{1,0:T(8,128)S(1)}, f32[8,1,768]{2,1,0:T(1,128)S(1)}) custom-call(f32[32,1,768]{2,1,0:T(1,128)S(1)} %all_to_all.32.p_ref, bf16[768,768]{1,0:T(8,128)(2,1)S(1)} %get-tuple-element.14.a_ref, bf16[768,768]{1,0:T(8,128)(2,1)S(1)} %get-tuple-element.15.g_ref, bf16[768,768]{1,0:T(8,128)(2,1)S(1)} %get-tuple-element.16.e_ref), custom_call_target="tpu_custom_call" | custom-call | tf_op jit(solution)/shard_map/right_term/pallas_call | solution.py:172
  55.5 7.4 %all_to_all.33.in_ref = f32[8,1,768]{2,1,0:T(1,128)S(1)} all-to-all(f32[8,1,768]{2,1,0:T(1,128)S(1)} %get-tuple-element.17), channel_id=1, replica_groups={{0,16,32,48,64,80,96,112},{128,144,160,176,192,208,224,240},{256,272,28..., dimensions={0} | all-to-all | bytes 49152 | tf_op jit(solution)/shard_map/all_to_all | solution.py:251
  63.0 14.0 %all_to_all.34.in_ref = f32[16,1,768]{2,1,0:T(1,128)S(1)} all-to-all(f32[16,1,768]{2,1,0:T(1,128)S(1)} %sum_parts.6), channel_id=1, replica_groups=mesh['inner'=32,'outer'=16] {'outer'}, dimensions={0} | all-to-all | bytes 98304 | tf_op jit(solution)/shard_map/all_to_all | solution.py:251
  77.0 12.4 %all_to_all.35.q_ref = f32[32,1,768]{2,1,0:T(1,128)S(1)} all-to-all(f32[32,1,768]{2,1,0:T(1,128)S(1)} %sum_parts.7), channel_id=1, replica_groups=mesh['inner'=32,'outer'=16] {'inner'}, dimensions={0} | all-to-all | bytes 196608 | tf_op jit(solution)/shard_map/all_to_all | solution.py:251
  89.5 1.4 %new_error.1 = (bf16[1,768,768]{2,1,0:T(8,128)(2,1)}, f32[8,768]{1,0:T(8,128)}, f32[8,768]{1,0:T(8,128)}) custom-call(f32[32,1,768]{2,1,0:T(1,128)S(1)} %all_to_all.35.q_ref, f32[8,768]{1,0:T(8,128)S(1)} %get-tuple-element.18.basis_ref, bf16[768,768]{1,0:T(8,128)(2,1)S(1)} %get-tuple-element.14.a_ref, bf16[768,768]{1,0:T(8,128)(2,1)S(1)} %get-tuple-element.15.g_ref, ...), custom_call_target="tpu_custom_call" | custom-call | tf_op jit(solution)/shard_map/new_error/pallas_call | solution.py:231
  (4 shorter events, 0.1 us)

commit v6 on v5

--- a/solution.py
+++ b/solution.py
@@ -7,6 +7,9 @@
 from jax.sharding import PartitionSpec as P
 
 BLOCK = 256
+PAIR = 2
+FIRST = ((1, 2), (3, 0))
+LAST = ((0, 1), (2, 3))
 BF16 = jnp.bfloat16
 F32 = jnp.float32
 TERMS = 3
@@ -54,8 +57,9 @@
 
 
 def store_parts(parts_ref, rows):
-    for at in range(rows.shape[0]):
-        parts_ref[at] = rows[at:at + 1]
+    copies = parts_ref.shape[0] // rows.shape[0]
+    for at in range(parts_ref.shape[0]):
+        parts_ref[at] = rows[at // copies:at // copies + 1]
 
 
 def sum_rows(parts_ref, rank):
@@ -104,7 +108,7 @@
             pltpu.VMEM(out_grads.shape, BF16),
             pltpu.VMEM(error.shape, BF16),
             pltpu.VMEM(error.shape, F32),
-            pltpu.VMEM((rank, 1, height), F32),
+            pltpu.VMEM((PAIR * rank, 1, height), F32),
         ),
         in_specs=[SPEC_ANY] * 4,
         out_specs=(SPEC_VMEM,) * 5,
@@ -158,7 +162,7 @@
 
 
 def right_kernel(p_ref, a_ref, g_ref, e_ref, basis_ref, parts_ref):
-    rank = parts_ref.shape[0]
+    rank = basis_ref.shape[0]
     rows = sum_rows(p_ref, rank)
     inverse = inverse_factor(rows)
     basis_ref[...] = combine(inverse, rows)
@@ -174,7 +178,7 @@
         name="right_term",
         out_shape=(
             pltpu.VMEM((rank, activations.shape[1]), F32),
-            pltpu.VMEM((rank, 1, out_grads.shape[1]), F32),
+            pltpu.VMEM((PAIR * rank, 1, out_grads.shape[1]), F32),
         ),
         in_specs=[SPEC_VMEM] * 4,
         out_specs=(SPEC_VMEM,) * 2,
@@ -252,12 +256,13 @@
 
 
 def reduce_all(parts):
-    rank = parts.shape[0]
-    n_inner, n_outer = lax.axis_size("inner"), lax.axis_size("outer")
-    groups = [list(range(first, first + rank)) for first in range(0, n_inner, rank)]
-    parts = sum_parts(exchange(parts, "inner", groups), n_outer)
-    parts = sum_parts(exchange(parts, "outer"), n_inner)
-    return exchange(parts, "inner")
+    rank = parts.shape[0] // PAIR
+    n_outer = lax.axis_size("outer")
+    within = [[x * rank + k for k in range(rank) for x in pair] for pair in FIRST]
+    across = [[x * rank + k for x in pair for k in range(rank)] for pair in LAST]
+    parts = sum_parts(exchange(parts, "inner", within), n_outer)
+    parts = sum_parts(exchange(parts, "outer"), PAIR * rank)
+    return exchange(parts, "inner", across)
 
 
 def local(activations, out_grads, error_in, q_init):

time: 91.2 us -> 90.4 us (level)
  no operation moved by 1% of the time
where the time goes in v6:
time: 90.4 us; the launch traced here: 90.1 us
  blocking collectives  83.1 us (92%)
  Pallas kernels  6.35 us (7%)
    all_to_all x6, blocking collectives, exchange(): return lax.all_to_all(parts, axis, 0, 0, axis_index_groups=groups)  83.1 us
    pallas_call x1, Pallas kernels, left_term(): pl.pallas_call(functools.partial(left_kernel, n_outer), name='left_term',...  3.88 us

profile of v6, /device:TPU:1, one launch (start us, length us, event | category | flops | bytes accessed | tf_op | source)
XLA Modules:
  0.0 90.1 jit_solution(14725952143322915350)
XLA Ops:
  0.6 3.9 %left_term.1 = (bf16[768,768]{1,0:T(8,128)(2,1)S(1)}, bf16[768,768]{1,0:T(8,128)(2,1)S(1)}, bf16[768,768]{1,0:T(8,128)(2,1)S(1)}, f32[768,768]{1,0:T(8,128)S(1)}, f32[16,1,768]{2,1,0:T(1,128)S(1)}) custom-call(bf16[768,768]{1,0:T(8,128)(2,1)} %a_hbm.1, bf16[768,768]{1,0:T(8,128)(2,1)} %g_hbm.1, bf16[768,768]{1,0:T(8,128)(2,1)} %bitcast.4, f32[8,768]{1,0:T(8,128)} %bitcast.5), custom_call_target="tpu_custom_call" | custom-call | tf_op jit(solution)/shard_map/left_term/pallas_call | solution.py:103
  4.5 15.7 %all_to_all.30.in_ref = f32[16,1,768]{2,1,0:T(1,128)S(1)} all-to-all(f32[16,1,768]{2,1,0:T(1,128)S(1)} %get-tuple-element.13), channel_id=1, replica_groups={{128,256,144,272,160,288,176,304,192,320,208,336,224,352,240,368},{384,..., dimensions={0} | all-to-all | bytes 98304 | tf_op jit(solution)/shard_map/all_to_all | solution.py:255
  20.3 22.5 %all_to_all.31.in_ref = f32[16,1,768]{2,1,0:T(1,128)S(1)} all-to-all(f32[16,1,768]{2,1,0:T(1,128)S(1)} %sum_parts.4), channel_id=1, replica_groups=mesh['inner'=32,'outer'=16] {'outer'}, dimensions={0} | all-to-all | bytes 98304 | tf_op jit(solution)/shard_map/all_to_all | solution.py:255
  42.8 10.4 %all_to_all.32.p_ref = f32[16,1,768]{2,1,0:T(1,128)S(1)} all-to-all(f32[16,1,768]{2,1,0:T(1,128)S(1)} %sum_parts.5), channel_id=1, replica_groups={{0,16,32,48,64,80,96,112,128,144,160,176,192,208,224,240},{256,272,288,..., dimensions={0} | all-to-all | bytes 98304 | tf_op jit(solution)/shard_map/all_to_all | solution.py:255
  53.1 1.0 %right_term.1 = (f32[8,768]{1,0:T(8,128)S(1)}, f32[16,1,768]{2,1,0:T(1,128)S(1)}) custom-call(f32[16,1,768]{2,1,0:T(1,128)S(1)} %all_to_all.32.p_ref, bf16[768,768]{1,0:T(8,128)(2,1)S(1)} %get-tuple-element.14.a_ref, bf16[768,768]{1,0:T(8,128)(2,1)S(1)} %get-tuple-element.15.g_ref, bf16[768,768]{1,0:T(8,128)(2,1)S(1)} %get-tuple-element.16.e_ref), custom_call_target="tpu_custom_call" | custom-call | tf_op jit(solution)/shard_map/right_term/pallas_call | solution.py:176
  54.1 10.0 %all_to_all.33.in_ref = f32[16,1,768]{2,1,0:T(1,128)S(1)} all-to-all(f32[16,1,768]{2,1,0:T(1,128)S(1)} %get-tuple-element.17), channel_id=1, replica_groups={{128,256,144,272,160,288,176,304,192,320,208,336,224,352,240,368},{384,..., dimensions={0} | all-to-all | bytes 98304 | tf_op jit(solution)/shard_map/all_to_all | solution.py:255
  64.1 14.1 %all_to_all.34.in_ref = f32[16,1,768]{2,1,0:T(1,128)S(1)} all-to-all(f32[16,1,768]{2,1,0:T(1,128)S(1)} %sum_parts.6), channel_id=1, replica_groups=mesh['inner'=32,'outer'=16] {'outer'}, dimensions={0} | all-to-all | bytes 98304 | tf_op jit(solution)/shard_map/all_to_all | solution.py:255
  78.3 10.4 %all_to_all.35.q_ref = f32[16,1,768]{2,1,0:T(1,128)S(1)} all-to-all(f32[16,1,768]{2,1,0:T(1,128)S(1)} %sum_parts.7), channel_id=1, replica_groups={{0,16,32,48,64,80,96,112,128,144,160,176,192,208,224,240},{256,272,288,..., dimensions={0} | all-to-all | bytes 98304 | tf_op jit(solution)/shard_map/all_to_all | solution.py:255
  88.7 1.4 %new_error.1 = (bf16[1,768,768]{2,1,0:T(8,128)(2,1)}, f32[8,768]{1,0:T(8,128)}, f32[8,768]{1,0:T(8,128)}) custom-call(f32[16,1,768]{2,1,0:T(1,128)S(1)} %all_to_all.35.q_ref, f32[8,768]{1,0:T(8,128)S(1)} %get-tuple-element.18.basis_ref, bf16[768,768]{1,0:T(8,128)(2,1)S(1)} %get-tuple-element.14.a_ref, bf16[768,768]{1,0:T(8,128)(2,1)S(1)} %get-tuple-element.15.g_ref, ...), custom_call_target="tpu_custom_call" | custom-call | tf_op jit(solution)/shard_map/new_error/pallas_call | solution.py:235
  (4 shorter events, 0.1 us)

commit v7 on v6

--- a/solution.py
+++ b/solution.py
@@ -255,11 +255,11 @@
     return lax.all_to_all(parts, axis, 0, 0, axis_index_groups=groups)
 
 
-def reduce_all(parts):
+def reduce_all(parts, first_pairs, last_pairs):
     rank = parts.shape[0] // PAIR
     n_outer = lax.axis_size("outer")
-    within = [[x * rank + k for k in range(rank) for x in pair] for pair in FIRST]
-    across = [[x * rank + k for x in pair for k in range(rank)] for pair in LAST]
+    within = [[x * rank + k for k in range(rank) for x in pair] for pair in first_pairs]
+    across = [[x * rank + k for x in pair for k in range(rank)] for pair in last_pairs]
     parts = sum_parts(exchange(parts, "inner", within), n_outer)
     parts = sum_parts(exchange(parts, "outer"), PAIR * rank)
     return exchange(parts, "inner", across)
@@ -269,8 +269,8 @@
     n_outer = lax.axis_size("outer")
     devices_all = lax.axis_size("inner") * n_outer
     *operands, merged, parts = left_term(activations, out_grads, error_in[0], q_init.T, n_outer)
-    basis_rows, parts = right_term(reduce_all(parts), *operands, q_init.shape[1])
-    error_out, q_rows, p_rows = new_error(reduce_all(parts), basis_rows, *operands, merged, n_outer, devices_all)
+    basis_rows, parts = right_term(reduce_all(parts, FIRST, LAST), *operands, q_init.shape[1])
+    error_out, q_rows, p_rows = new_error(reduce_all(parts, LAST, FIRST), basis_rows, *operands, merged, n_outer, devices_all)
     return (error_out, p_rows.T, q_rows.T)
 
 

time: 90.4 us -> 89.9 us (level)
  no operation moved by 1% of the time
where the time goes in v7:
time: 89.9 us; the launch traced here: 89.6 us
  blocking collectives  82.6 us (92%)
  Pallas kernels  6.36 us (7%)
    all_to_all x6, blocking collectives, exchange(): return lax.all_to_all(parts, axis, 0, 0, axis_index_groups=groups)  82.6 us
    pallas_call x1, Pallas kernels, left_term(): pl.pallas_call(functools.partial(left_kernel, n_outer), name='left_term',...  3.88 us

profile of v7, /device:TPU:1, one launch (start us, length us, event | category | flops | bytes accessed | tf_op | source)
XLA Modules:
  0.0 89.6 jit_solution(9590577214018580915)
XLA Ops:
  0.6 3.9 %left_term.1 = (bf16[768,768]{1,0:T(8,128)(2,1)S(1)}, bf16[768,768]{1,0:T(8,128)(2,1)S(1)}, bf16[768,768]{1,0:T(8,128)(2,1)S(1)}, f32[768,768]{1,0:T(8,128)S(1)}, f32[16,1,768]{2,1,0:T(1,128)S(1)}) custom-call(bf16[768,768]{1,0:T(8,128)(2,1)} %a_hbm.1, bf16[768,768]{1,0:T(8,128)(2,1)} %g_hbm.1, bf16[768,768]{1,0:T(8,128)(2,1)} %bitcast.4, f32[8,768]{1,0:T(8,128)} %bitcast.5), custom_call_target="tpu_custom_call" | custom-call | tf_op jit(solution)/shard_map/left_term/pallas_call | solution.py:103
  4.5 15.7 %all_to_all.30.in_ref = f32[16,1,768]{2,1,0:T(1,128)S(1)} all-to-all(f32[16,1,768]{2,1,0:T(1,128)S(1)} %get-tuple-element.13), channel_id=1, replica_groups={{128,256,144,272,160,288,176,304,192,320,208,336,224,352,240,368},{384,..., dimensions={0} | all-to-all | bytes 98304 | tf_op jit(solution)/shard_map/all_to_all | solution.py:255
  20.3 22.5 %all_to_all.31.in_ref = f32[16,1,768]{2,1,0:T(1,128)S(1)} all-to-all(f32[16,1,768]{2,1,0:T(1,128)S(1)} %sum_parts.4), channel_id=1, replica_groups=mesh['inner'=32,'outer'=16] {'outer'}, dimensions={0} | all-to-all | bytes 98304 | tf_op jit(solution)/shard_map/all_to_all | solution.py:255
  42.8 10.4 %all_to_all.32.p_ref = f32[16,1,768]{2,1,0:T(1,128)S(1)} all-to-all(f32[16,1,768]{2,1,0:T(1,128)S(1)} %sum_parts.5), channel_id=1, replica_groups={{0,16,32,48,64,80,96,112,128,144,160,176,192,208,224,240},{256,272,288,..., dimensions={0} | all-to-all | bytes 98304 | tf_op jit(solution)/shard_map/all_to_all | solution.py:255
  53.1 1.0 %right_term.1 = (f32[8,768]{1,0:T(8,128)S(1)}, f32[16,1,768]{2,1,0:T(1,128)S(1)}) custom-call(f32[16,1,768]{2,1,0:T(1,128)S(1)} %all_to_all.32.p_ref, bf16[768,768]{1,0:T(8,128)(2,1)S(1)} %get-tuple-element.14.a_ref, bf16[768,768]{1,0:T(8,128)(2,1)S(1)} %get-tuple-element.15.g_ref, bf16[768,768]{1,0:T(8,128)(2,1)S(1)} %get-tuple-element.16.e_ref), custom_call_target="tpu_custom_call" | custom-call | tf_op jit(solution)/shard_map/right_term/pallas_call | solution.py:176
  54.1 8.7 %all_to_all.33.in_ref = f32[16,1,768]{2,1,0:T(1,128)S(1)} all-to-all(f32[16,1,768]{2,1,0:T(1,128)S(1)} %get-tuple-element.17), channel_id=1, replica_groups={{0,128,16,144,32,160,48,176,64,192,80,208,96,224,112,240},{256,384,272,..., dimensions={0} | all-to-all | bytes 98304 | tf_op jit(solution)/shard_map/all_to_all | solution.py:255
  62.9 14.1 %all_to_all.34.in_ref = f32[16,1,768]{2,1,0:T(1,128)S(1)} all-to-all(f32[16,1,768]{2,1,0:T(1,128)S(1)} %sum_parts.6), channel_id=1, replica_groups=mesh['inner'=32,'outer'=16] {'outer'}, dimensions={0} | all-to-all | bytes 98304 | tf_op jit(solution)/shard_map/all_to_all | solution.py:255
  77.0 11.1 %all_to_all.35.q_ref = f32[16,1,768]{2,1,0:T(1,128)S(1)} all-to-all(f32[16,1,768]{2,1,0:T(1,128)S(1)} %sum_parts.7), channel_id=1, replica_groups={{128,144,160,176,192,208,224,240,256,272,288,304,320,336,352,368},{384,..., dimensions={0} | all-to-all | bytes 98304 | tf_op jit(solution)/shard_map/all_to_all | solution.py:255
  88.2 1.4 %new_error.1 = (bf16[1,768,768]{2,1,0:T(8,128)(2,1)}, f32[8,768]{1,0:T(8,128)}, f32[8,768]{1,0:T(8,128)}) custom-call(f32[16,1,768]{2,1,0:T(1,128)S(1)} %all_to_all.35.q_ref, f32[8,768]{1,0:T(8,128)S(1)} %get-tuple-element.18.basis_ref, bf16[768,768]{1,0:T(8,128)(2,1)S(1)} %get-tuple-element.14.a_ref, bf16[768,768]{1,0:T(8,128)(2,1)S(1)} %get-tuple-element.15.g_ref, ...), custom_call_target="tpu_custom_call" | custom-call | tf_op jit(solution)/shard_map/new_error/pallas_call | solution.py:235
  (4 shorter events, 0.1 us)
